TPU v7x, 32 devices: a whole 2x2x4 slice. The times are simulated.
32 devices in a mesh: ctx: 8 (over z, x), fsdp: 4 (over y, core).
Axes of the slice: x: 2, y: 2, z: 4, core: 2. Of those that a mesh axis runs over, the one named last changes fastest.
Arguments:
- tokens: bfloat16 [4, 2048, 8192], P('fsdp', 'ctx'), may hold values from -6 to 6
- queries: bfloat16 [4, 2048, 8192], P('fsdp', 'ctx'), may hold values from -384 to 384
- kv_weight: bfloat16 [8192, 2048], P(None, 'fsdp'), may hold values from -0.0625 to 0.0625
- block_list: int32 [8, 16, 8], replicated, may hold values from 0 to 15, as said below
- counts: int32 [8, 16], replicated, may hold values from 4 to 8, as said below
Outputs:
- attended: bfloat16 [4, 2048, 8192], P('fsdp', 'ctx')
Inputs may be any that keep to these rules, and one draw needn't show every extreme that they name: `block_list`: for each g and b the first counts[g, b] entries are distinct: block b, blocks b - 1 and b + 1 modulo 16 (the window wraps at the sequence's ends), the two global blocks of group g, and random blocks; the later entries are further distinct blocks. `counts`: some list has 8 live entries in every draw; loads differ from group to group.
All inputs are finite; a program needn't handle non-finite values.
Results may differ from a plain program's by a relative error of at most 0.007.
The roundings to bfloat16 on the way count: a program that leaves them out, or rounds other values in their place, can miss the bound.
Values may be sent and summed in bfloat16 or wider, within the bound.
No kernel may reach another device: no remote copies, remote signals or barrier semaphores. Data moves between devices by JAX's collectives and lax.ppermute only.
A program may use at most 192 MiB of HBM per device.

v0:
```python
import functools

import jax
import jax.numpy as jnp
from jax import lax
from jax.experimental import pallas as pl
from jax.experimental.pallas import tpu as pltpu
from jax.sharding import PartitionSpec as P

DH = 128
BLK = 128
PAIR = 2 * DH
GROUP_HEADS = 8
GROUP_WIDTH = GROUP_HEADS * DH
LOG2E = 1.4426950408889634
SHARES = (8, 5, 3)

KERNEL_VMEM = 48 << 20
COST = pl.CostEstimate(flops=1, bytes_accessed=1, transcendentals=0)


def swap(array, axis, bit):
    size = lax.axis_size(axis)
    return lax.ppermute(array, axis, [(i, i ^ bit) for i in range(size)])


def rotate(array, steps, column_bit=0):
    n_ctx, n_col = lax.axis_size("ctx"), lax.axis_size("fsdp")
    order = []
    for c in range(n_ctx):
        to = (c + 2 * steps) % n_ctx
        order += [(c * n_col + f, to * n_col + (f ^ column_bit)) for f in range(n_col)]
    return lax.ppermute(array, ("ctx", "fsdp"), order)


def pin(mark, *arrays):
    return lax.optimization_barrier((mark, *arrays))


def cut_kernel(start, in_ref, out_ref, sem):
    copy = pltpu.make_async_copy(in_ref.at[pl.ds(start, out_ref.shape[0])], out_ref, sem)
    copy.start()
    copy.wait()


def cut(array, start, rows):
    return pl.pallas_call(
        functools.partial(cut_kernel, start),
        out_shape=jax.ShapeDtypeStruct((rows, array.shape[1]), array.dtype),
        in_specs=[pl.BlockSpec(memory_space=pltpu.HBM)],
        out_specs=pl.BlockSpec(memory_space=pltpu.VMEM),
        scratch_shapes=[pltpu.SemaphoreType.DMA],
        cost_estimate=COST,
        compiler_params=pltpu.CompilerParams(vmem_limit_bytes=8 << 20),
    )(array)


def turn_steps():
    pairs = lax.axis_size("ctx") // 2
    return sorted(range(1, pairs), key=lambda r: min(r, pairs - r))


def turn_all(array):
    return [rotate(array, r) for r in turn_steps()]


def cross(array):
    return swap(array, "ctx", 1)


def project_kernel(n_weights, tile, row_ref, *refs):
    weight_refs = refs[:n_weights]
    out_ref, held, total, sems = refs[-4:]
    width = weight_refs[0].shape[1]
    depth = row_ref.shape[1]
    copies = []
    for k in range(depth // tile):
        for i in range(n_weights):
            copies.append(
                pltpu.make_async_copy(
                    weight_refs[i].at[pl.ds(k * tile, tile)],
                    held.at[i, pl.ds(k * tile, tile)],
                    sems.at[k * n_weights + i],
                )
            )
    for copy in copies:
        copy.start()
    for k in range(depth // tile):
        for i in range(n_weights):
            copies[k * n_weights + i].wait()
            product = jnp.dot(
                row_ref[:, k * tile : (k + 1) * tile],
                held[i, k * tile : (k + 1) * tile, :],
                preferred_element_type=jnp.float32,
            )
            columns = slice(i * width, (i + 1) * width)
            if k == 0:
                total[:, columns] = product
            elif k + 1 < depth // tile:
                total[:, columns] += product
            else:
                out_ref[:, columns] = (total[:, columns] + product).astype(jnp.bfloat16)


def project(rows, weights):
    n_rows, depth = rows.shape
    width = weights[0].shape[1]
    tile = 1024
    n_weights = len(weights)
    out_width = width * n_weights
    inside = pl.BlockSpec(memory_space=pltpu.VMEM)
    return pl.pallas_call(
        functools.partial(project_kernel, n_weights, tile),
        out_shape=jax.ShapeDtypeStruct((n_rows, out_width), jnp.bfloat16),
        in_specs=[inside] + [pl.BlockSpec(memory_space=pltpu.HBM)] * n_weights,
        out_specs=inside,
        scratch_shapes=[
            pltpu.VMEM((n_weights, depth, width), jnp.bfloat16),
            pltpu.VMEM((n_rows, out_width), jnp.float32),
            pltpu.SemaphoreType.DMA((depth // tile * n_weights,)),
        ],
        cost_estimate=COST,
        compiler_params=pltpu.CompilerParams(vmem_limit_bytes=KERNEL_VMEM),
    )(rows, *weights)


def attend_blocks(live, q_ref, row_at, state_at, key_rows, value_rows, state_in, results):
    scale = DH ** (-0.5) * LOG2E
    keys = key_rows[: live * BLK, :]
    values = value_rows[: live * BLK, :].astype(jnp.float32).T.astype(jnp.bfloat16)
    for head in range(GROUP_HEADS):
        columns = slice(head * DH, (head + 1) * DH)
        q = q_ref[pl.ds(row_at, BLK), columns]
        scores = lax.dot_general(
            keys, q, (((1,), (1,)), ((), ())), preferred_element_type=jnp.float32
        )
        top = jnp.max(scores, axis=0, keepdims=True)
        weights = jnp.exp2((scores - top) * scale)
        total = jnp.sum(weights, axis=0, keepdims=True)
        mixed = jnp.dot(values, weights.astype(jnp.bfloat16), preferred_element_type=jnp.float32)
        if len(results) == 2:
            results[0][state_at * GROUP_HEADS + head] = mixed
            results[1][state_at * GROUP_HEADS + head, 0:1] = top
            results[1][state_at * GROUP_HEADS + head, 1:2] = total
            continue
        if state_in:
            other = state_in[1][state_at * GROUP_HEADS + head]
            other_top, other_total = other[0:1], other[1:2]
            both = jnp.maximum(top, other_top)
            here, there = jnp.exp2((top - both) * scale), jnp.exp2((other_top - both) * scale)
            total = total * here + other_total * there
            mixed = mixed * here + state_in[0][state_at * GROUP_HEADS + head] * there
        results[0][pl.ds(row_at, BLK), columns] = (mixed / total).T.astype(jnp.bfloat16)


def attend_kernel(places, shape, first_group, part, resumes, group_ref, list_ref, count_ref, me_ref, q_ref, *refs):
    held, q_held, key_rows, value_rows, sems = refs[-5:]
    blocks, max_live, local_blocks = shape
    state_in = refs[len(places) : len(places) + 2] if resumes else ()
    results = refs[-7:-5] if part == 0 else refs[-6:-5]
    held_rows = local_blocks * BLK if part is None else BLK
    pairs = held.shape[1] // (2 * held_rows)
    step, me = pl.program_id(0), me_ref[0]
    n_steps = pl.num_programs(0)

    def copies(index, slot):
        q_at = pl.multiple_of(group_ref[index] * GROUP_WIDTH, GROUP_WIDTH)
        made = [
            pltpu.make_async_copy(
                q_ref.at[:, pl.ds(q_at, GROUP_WIDTH)], q_held.at[slot], sems.at[slot, 0]
            )
        ]
        columns = pl.ds(pl.multiple_of((first_group + index) * PAIR, PAIR), PAIR)
        for ref, place in zip(refs, places):
            at = 0
            for back, member, row_at, rows in place:
                pair = lax.rem(me // 2 + pairs - back, pairs)
                start = pl.multiple_of((2 * pair + member) * held_rows + row_at, 16)
                made.append(
                    pltpu.make_async_copy(
                        ref.at[pl.ds(at, rows), columns],
                        held.at[slot, pl.ds(start, rows)],
                        sems.at[slot, len(made)],
                    )
                )
                at += rows
        return made

    slot = lax.rem(step, 2)

    @pl.when(step == 0)
    def _():
        for copy in copies(step, slot):
            copy.start()

    @pl.when(step + 1 < n_steps)
    def _():
        for copy in copies(step + 1, 1 - slot):
            copy.start()

    for copy in copies(step, slot):
        copy.wait()

    def one_block(block, carry):
        row_at = pl.multiple_of(block * BLK, BLK)
        entry = group_ref[step] * blocks + me * local_blocks + block
        count = count_ref[entry]
        taken = jnp.int32(0)
        for j in range(max_live):
            listed = list_ref[entry * max_live + j]
            source, inside = listed // local_blocks, lax.rem(listed, local_blocks)
            member = lax.rem(source + me, 2)
            from_row = (source // 2 * 2 + member) * held_rows
            wanted = j < count
            if part is None:
                from_row += inside * BLK
            else:
                wanted = jnp.logical_and(wanted, inside == part)
            from_row = pl.multiple_of(from_row, BLK)
            to_row = pl.multiple_of(taken * BLK, BLK)

            @pl.when(wanted)
            def _(from_row=from_row, to_row=to_row):
                chosen = held[slot, pl.ds(from_row, BLK), :]
                key_rows[pl.ds(to_row, BLK), :] = chosen[:, :DH]
                value_rows[pl.ds(to_row, BLK), :] = chosen[:, DH:]

            taken = taken + wanted.astype(jnp.int32)
        for live in range(4, max_live + 1) if part is None else range(1, max_live):
            pl.when(taken == live)(
                functools.partial(
                    attend_blocks,
                    live,
                    q_held.at[slot],
                    row_at,
                    block,
                    key_rows,
                    value_rows,
                    state_in,
                    results,
                )
            )
        return carry

    lax.fori_loop(0, local_blocks, one_block, 0)


def attend(queries, pieces, groups, first_group, block_list, counts, so_far, part=None, state=()):
    n_groups = groups.shape[0]
    rows, width = queries.shape
    local_blocks = rows // BLK
    blocks, max_live = block_list.shape[1:]
    places = [parts for _, parts in pieces]
    held_rows = sum(entry[-1] for parts in places for entry in parts)
    n_copies = 1 + sum(len(parts) for parts in places)
    me = lax.axis_index("ctx").astype(jnp.int32).reshape(1)
    anywhere = pl.BlockSpec(memory_space=pltpu.HBM)
    scalars = [groups, block_list.reshape(-1), counts.reshape(-1), me]
    operands = [queries] + [p for p, _ in pieces]
    in_specs = [anywhere] * len(operands)
    state_shapes = [
        (n_groups * local_blocks * GROUP_HEADS, DH, BLK),
        (n_groups * local_blocks * GROUP_HEADS, 8, BLK),
    ]
    state_specs = [
        pl.BlockSpec((local_blocks * GROUP_HEADS, *shape[1:]), lambda i, *_: (i, 0, 0))
        for shape in state_shapes
    ]
    operands += state
    in_specs += state_specs[: len(state)]
    aliases = {}
    if so_far is not None:
        aliases = {len(scalars) + len(operands): 0}
        operands.append(so_far)
        in_specs.append(anywhere)
    if part == 0:
        out_shape = [jax.ShapeDtypeStruct(shape, jnp.float32) for shape in state_shapes]
        out_specs = state_specs
    else:
        out_shape = jax.ShapeDtypeStruct((rows, width), jnp.bfloat16)
        out_specs = pl.BlockSpec((rows, GROUP_WIDTH), lambda i, g, *_: (0, g[i]))
    return pl.pallas_call(
        functools.partial(
            attend_kernel, places, (blocks, max_live, local_blocks), first_group, part, bool(state)
        ),
        out_shape=out_shape,
        grid_spec=pltpu.PrefetchScalarGridSpec(
            num_scalar_prefetch=len(scalars),
            grid=(n_groups,),
            in_specs=in_specs,
            out_specs=out_specs,
            scratch_shapes=[
                pltpu.VMEM((2, held_rows, PAIR), jnp.bfloat16),
                pltpu.VMEM((2, rows, GROUP_WIDTH), jnp.bfloat16),
                pltpu.VMEM((max_live * BLK, DH), jnp.bfloat16),
                pltpu.VMEM((max_live * BLK, DH), jnp.bfloat16),
                pltpu.SemaphoreType.DMA((2, n_copies)),
            ],
        ),
        input_output_aliases=aliases,
        cost_estimate=COST,
        compiler_params=pltpu.CompilerParams(vmem_limit_bytes=60 << 20),
    )(*scalars, *operands)


def on_device(tokens, queries, kv_weight, block_list, counts):
    rows = tokens.shape[1]
    tokens = tokens.reshape(rows, -1)
    queries = queries.reshape(rows, -1)
    col = lax.axis_index("fsdp")
    local_groups = kv_weight.shape[1] // PAIR

    def groups_of(column):
        return column * local_groups + jnp.arange(local_groups, dtype=jnp.int32)

    def attend_to(groups, pieces, half, so_far, part=None, state=()):
        at = half * local_groups
        return attend(queries, pieces, groups, at, block_list, counts, so_far, part, state)

    def line(arrays, backs, place, member):
        return [(p, [(r, member, *place)]) for r, p in zip(backs, arrays)]

    at_second = SHARES[0] * rows // 16
    at_last = (SHARES[0] + SHARES[1]) * rows // 16
    n_turned = at_last - at_second
    steps = turn_steps()
    whole, early = (0, rows), (0, at_second)
    middle, late = (at_second, n_turned), (at_last, rows - at_last)
    pairs = lax.axis_size("ctx") // 2
    mark = jnp.zeros((8, 128), jnp.float32)

    first_got = swap(cut(tokens, 0, at_second), "fsdp", 2)
    second_out = tokens[at_second:]
    near_weight = swap(kv_weight, "fsdp", 1)
    own = project(tokens, (kv_weight,))

    mark, own, second_out = pin(mark, own, second_out)
    own_turned = turn_all(own)
    near = project(tokens, (near_weight,))
    mark, near, *own_turned = pin(mark, near, *own_turned)
    own_line = [own, *own_turned]
    own_crossed = cross(jnp.concatenate(own_line, axis=0))
    near_turned = turn_all(near)
    second_got = swap(second_out, "fsdp", 2)
    mark, first_got, own_crossed = pin(mark, first_got, own_crossed)

    def side_pieces(pieces, crossed):
        return line(pieces, [0, *steps], whole, 0) + [(crossed, [(r, 1, *whole) for r in [0, *steps]])]

    first = project(first_got, (kv_weight, near_weight))
    mark, first, *near_turned = pin(mark, first, *near_turned)
    first = rotate(first, 1, 2)
    near_line = [near, *near_turned]
    near_crossed = cross(jnp.concatenate(near_line, axis=0))
    mark, first = pin(mark, first)
    first_turned = turn_all(first)
    first_backs = [(1 + r) % pairs for r in [0, *steps]]
    out = attend_to(groups_of(col), side_pieces(own_line, own_crossed), 0, None)

    mark, out, near_crossed, *first_turned = pin(mark, out, near_crossed, *first_turned)
    first_crossed = cross(jnp.concatenate([first, *first_turned], axis=0))
    mark, second_got = pin(mark, second_got)
    second = project(second_got, (kv_weight, near_weight))
    mark, second = pin(mark, second)
    back = swap(second, "fsdp", 2)
    turned = [rotate(second[:n_turned], r, 2) for r in steps]
    mark, back = pin(mark, back)
    last_crossed = cross(back[n_turned:])

    mark, last_crossed, first_crossed, *turned = pin(mark, last_crossed, first_crossed, *turned)
    crossed = cross(jnp.concatenate([back[:n_turned], *turned], axis=0))
    last_pair = jnp.concatenate([back[n_turned:], last_crossed], axis=0)
    pair_turned = turn_all(last_pair)

    out = attend_to(groups_of(col ^ 1), side_pieces(near_line, near_crossed), 0, out)
    mark, out, crossed, *pair_turned = pin(mark, out, crossed, *pair_turned)

    far_pieces = line([first, *first_turned], first_backs, early, 0)
    far_pieces.append((first_crossed, [(r, 1, *early) for r in first_backs]))
    far_pieces += line([back[:n_turned], *turned], [0, *steps], middle, 0)
    far_pieces.append((crossed, [(r, 1, *middle) for r in [0, *steps]]))
    for r, piece in zip([0, *steps], [last_pair, *pair_turned]):
        far_pieces.append((piece, [(r, 0, *late), (r, 1, *late)]))
    far_groups = jnp.concatenate([groups_of(col ^ 2), groups_of(col ^ 3)])
    out = attend_to(far_groups, far_pieces, 0, out)
    return out.reshape(1, rows, -1)


def solution(mesh):
    return jax.shard_map(
        on_device,
        mesh=mesh,
        in_specs=(P("fsdp", "ctx", None), P("fsdp", "ctx", None), P(None, "fsdp"), P(), P()),
        out_specs=P("fsdp", "ctx", None),
        check_vma=False,
    )
```

profile of v0, /device:TPU:0, one launch (start us, length us, event | category | flops | bytes accessed | tf_op | source)
XLA Modules:
  0.0 175.5 jit_solution(2179107782552263831)
XLA Ops:
  0.5 2.2 %copy-done = bf16[1,256,8192]{2,1,0:T(8,128)(2,1)S(1)} copy-done((bf16[1,256,8192]{2,1,0:T(8,128)(2,1)S(1)}, bf16[1,256,8192]{2,1,0:T(8,128)(2,1)}, u32[]{:S(2)}) %copy-start) | copy-done | bytes 4194328
  2.8 2.6 %collective-permute-start = (bf16[128,8192]{1,0:T(8,128)(2,1)S(1)}, bf16[128,8192]{1,0:T(8,128)(2,1)S(1)}, u32[]{:S(2)}, u32[]{:S(2)}) collective-permute-start(bf16[128,8192]{1,0:T(8,128)(2,1)S(1)} %shard_map.55), channel_id=1, source_target_pairs={{0,2},{1,3},{2,0},{3,1},{4,6},{5,7},{6,4},{7,5},{8,10},{9,11},{10,... | collective-permute-start | bytes 6291464 | tf_op jit(solution)/shard_map/ppermute | solution.py:24
  5.4 1.5 slice_bitcast_fusion
  6.9 4.0 %shard_map.56.refs_0_ = bf16[256,512]{1,0:T(8,128)(2,1)S(1)} custom-call(bf16[256,8192]{1,0:T(8,128)(2,1)S(1)} %bitcast.7, bf16[8192,512]{1,0:T(8,128)(2,1)} %refs_0_.5), custom_call_target="tpu_custom_call" | custom-call | flops 1 | bytes 1 | tf_op jit(solution)/shard_map/pallas_call | solution.py:112
  10.9 3.1 %collective-permute-start.4 = (bf16[256,512]{1,0:T(8,128)(2,1)S(1)}, bf16[256,512]{1,0:T(8,128)(2,1)S(1)}, u32[]{:S(2)}, u32[]{:S(2)}) collective-permute-start(bf16[256,512]{1,0:T(8,128)(2,1)S(1)} %shard_map.56.refs_0_), channel_id=1, source_target_pairs={{0,16},{1,17},{2,18},{3,19},{4,20},{5,21},{6,22},{7,23},{8,24},{9,... | collective-permute-start | bytes 786440 | tf_op jit(solution)/shard_map/ppermute | solution.py:33
  16.0 4.0 %shard_map.57.refs_0_ = bf16[256,512]{1,0:T(8,128)(2,1)S(1)} custom-call(bf16[256,8192]{1,0:T(8,128)(2,1)S(1)} %bitcast.8, bf16[8192,512]{1,0:T(8,128)(2,1)} %collective-permute-done.1.refs_0_.refs_1_), custom_call_target="tpu_custom_call" | custom-call | flops 1 | bytes 1 | tf_op jit(solution)/shard_map/pallas_call | solution.py:112
  20.0 6.8 %collective-permute-done.4.refs_3_ = bf16[256,512]{1,0:T(8,128)(2,1)S(1)} collective-permute-done((bf16[256,512]{1,0:T(8,128)(2,1)S(1)}, bf16[256,512]{1,0:T(8,128)(2,1)S(1)}, u32[]{:S(2)}, u32[]{:S(2)}) %collective-permute-start.4) | collective-permute-done | bytes 262176 | tf_op jit(solution)/shard_map/ppermute | solution.py:33
  26.9 6.5 %collective-permute-done.2.refs_1_ = bf16[256,512]{1,0:T(8,128)(2,1)S(1)} collective-permute-done((bf16[256,512]{1,0:T(8,128)(2,1)S(1)}, bf16[256,512]{1,0:T(8,128)(2,1)S(1)}, u32[]{:S(2)}, u32[]{:S(2)}) %collective-permute-start.2) | collective-permute-done | bytes 262176 | tf_op jit(solution)/shard_map/ppermute | solution.py:33
  33.5 1.6 collective-permute-start.5
  35.1 7.1 %collective-permute-start.8 = (bf16[256,512]{1,0:T(8,128)(2,1)S(1)}, bf16[256,512]{1,0:T(8,128)(2,1)S(1)}, u32[]{:S(2)}, u32[]{:S(2)}) collective-permute-start(bf16[256,512]{1,0:T(8,128)(2,1)S(1)} %shard_map.57.refs_0_), channel_id=1, source_target_pairs={{0,16},{1,17},{2,18},{3,19},{4,20},{5,21},{6,22},{7,23},{8,24},{9,... | collective-permute-start | bytes 786440 | tf_op jit(solution)/shard_map/ppermute | solution.py:33
  42.6 1.6 collective-permute-start.6
  44.2 7.5 %collective-permute-done.row_ref = bf16[128,8192]{1,0:T(8,128)(2,1)S(1)} collective-permute-done((bf16[128,8192]{1,0:T(8,128)(2,1)S(1)}, bf16[128,8192]{1,0:T(8,128)(2,1)S(1)}, u32[]{:S(2)}, u32[]{:S(2)}) %collective-permute-start) | collective-permute-done | bytes 2097184 | tf_op jit(solution)/shard_map/ppermute | solution.py:24
  51.7 1.7 collective-permute-start.14
  53.4 4.9 %collective-permute-done.5.refs_4_ = bf16[1024,512]{1,0:T(8,128)(2,1)S(1)} collective-permute-done((bf16[1024,512]{1,0:T(8,128)(2,1)S(1)}, bf16[1024,512]{1,0:T(8,128)(2,1)S(1)}, u32[]{:S(2)}, u32[]{:S(2)}) %collective-permute-start.5) | collective-permute-done | bytes 1048608 | tf_op jit(solution)/shard_map/ppermute | solution.py:24
  58.3 6.6 %shard_map.58 = bf16[128,1024]{1,0:T(8,128)(2,1)S(1)} custom-call(bf16[128,8192]{1,0:T(8,128)(2,1)S(1)} %collective-permute-done.row_ref, bf16[8192,512]{1,0:T(8,128)(2,1)} %refs_0_.5, bf16[8192,512]{1,0:T(8,128)(2,1)} %collective-permute-done.1.refs_0_.refs_1_), custom_call_target="tpu_custom_call" | custom-call | flops 1 | bytes 1 | tf_op jit(solution)/shard_map/pallas_call | solution.py:112
  66.2 1.5 collective-permute-start.10
  67.7 6.5 %collective-permute-start.9 = (bf16[128,1024]{1,0:T(8,128)(2,1)S(1)}, bf16[128,1024]{1,0:T(8,128)(2,1)S(1)}, u32[]{:S(2)}, u32[]{:S(2)}) collective-permute-start(bf16[128,1024]{1,0:T(8,128)(2,1)S(1)} %shard_map.58), channel_id=1, source_target_pairs={{0,10},{1,11},{2,8},{3,9},{4,14},{5,15},{6,12},{7,13},{8,18},{9,19... | collective-permute-start | bytes 786440 | tf_op jit(solution)/shard_map/ppermute | solution.py:33
  74.2 4.7 %collective-permute-done.9.refs_0_ = bf16[128,1024]{1,0:T(8,128)(2,1)S(1)} collective-permute-done((bf16[128,1024]{1,0:T(8,128)(2,1)S(1)}, bf16[128,1024]{1,0:T(8,128)(2,1)S(1)}, u32[]{:S(2)}, u32[]{:S(2)}) %collective-permute-start.9) | collective-permute-done | bytes 262176 | tf_op jit(solution)/shard_map/ppermute | solution.py:33
  78.9 4.4 %collective-permute-start.13 = (bf16[128,1024]{1,0:T(8,128)(2,1)S(1)}, bf16[128,1024]{1,0:T(8,128)(2,1)S(1)}, u32[]{:S(2)}, u32[]{:S(2)}) collective-permute-start(bf16[128,1024]{1,0:T(8,128)(2,1)S(1)} %collective-permute-done.9.refs_0_), channel_id=1, source_target_pairs={{0,16},{1,17},{2,18},{3,19},{4,20},{5,21},{6,22},{7,23},{8,24},{9,... | collective-permute-start | bytes 786440 | tf_op jit(solution)/shard_map/ppermute | solution.py:33
  83.8 1.6 collective-permute-start.11
  87.3 9.1 %shard_map.59.refs_5_ = bf16[256,8192]{1,0:T(8,128)(2,1)} custom-call(s32[2]{0:T(128)} %iota_add_fusion.1.group_ref, s32[1024]{0:T(1024)} %reshape.25.list_ref, s32[128]{0:T(128)} %reshape.26.count_ref, s32[1]{0:T(128)} %bitcast.me_ref, bf16[256,8192]{1,0:T(8,128)(2,1)} %bitcast.9, bf16[256,512]{1,0:T(8,128)(2,1)} %copy-done.3, bf16[256,512]{1,0:T(8,128)(2,1)} %copy-done.14, ...), custom_call_target="tpu_custom_call" | custom-call | flops 1 | bytes 1 | tf_op jit(solution)/shard_map/pallas_call | solution.py:282
  96.5 2.9 %collective-permute-done.13.refs_3_ = bf16[128,1024]{1,0:T(8,128)(2,1)S(1)} collective-permute-done((bf16[128,1024]{1,0:T(8,128)(2,1)S(1)}, bf16[128,1024]{1,0:T(8,128)(2,1)S(1)}, u32[]{:S(2)}, u32[]{:S(2)}) %collective-permute-start.13) | collective-permute-done | bytes 262176 | tf_op jit(solution)/shard_map/ppermute | solution.py:33
  102.1 2.9 %collective-permute-done.14.row_ref = bf16[128,8192]{1,0:T(8,128)(2,1)S(1)} collective-permute-done((bf16[128,8192]{1,0:T(8,128)(2,1)}, bf16[128,8192]{1,0:T(8,128)(2,1)S(1)}, u32[]{:S(2)}, u32[]{:S(2)}) %collective-permute-start.14) | collective-permute-done | bytes 2097184 | tf_op jit(solution)/shard_map/ppermute | solution.py:24
  105.0 6.3 %shard_map.60 = bf16[128,1024]{1,0:T(8,128)(2,1)S(1)} custom-call(bf16[128,8192]{1,0:T(8,128)(2,1)S(1)} %collective-permute-done.14.row_ref, bf16[8192,512]{1,0:T(8,128)(2,1)} %refs_0_.5, bf16[8192,512]{1,0:T(8,128)(2,1)} %collective-permute-done.1.refs_0_.refs_1_), custom_call_target="tpu_custom_call" | custom-call | flops 1 | bytes 1 | tf_op jit(solution)/shard_map/pallas_call | solution.py:112
  111.3 1.6 collective-permute-start.15
  112.9 3.4 %collective-permute-start.20 = (bf16[80,1024]{1,0:T(8,128)(2,1)S(1)}, bf16[80,1024]{1,0:T(8,128)(2,1)S(1)}, u32[]{:S(2)}, u32[]{:S(2)}) collective-permute-start(bf16[80,1024]{1,0:T(8,128)(2,1)S(1)} %slice.25), channel_id=1, source_target_pairs={{0,18},{1,19},{2,16},{3,17},{4,22},{5,23},{6,20},{7,21},{8,26},{9,... | collective-permute-start | bytes 491528 | tf_op jit(solution)/shard_map/ppermute | solution.py:33
  116.2 2.1 %collective-permute-start.19 = (bf16[80,1024]{1,0:T(8,128)(2,1)S(1)}, bf16[80,1024]{1,0:T(8,128)(2,1)S(1)}, u32[]{:S(2)}, u32[]{:S(2)}) collective-permute-start(bf16[80,1024]{1,0:T(8,128)(2,1)S(1)} %slice.25), channel_id=1, source_target_pairs={{0,26},{1,27},{2,24},{3,25},{4,30},{5,31},{6,28},{7,29},{8,2},{9,3... | collective-permute-start | bytes 491528 | tf_op jit(solution)/shard_map/ppermute | solution.py:33
  119.2 10.0 %collective-permute-done.15 = bf16[128,1024]{1,0:T(8,128)(2,1)S(1)} collective-permute-done((bf16[128,1024]{1,0:T(8,128)(2,1)S(1)}, bf16[128,1024]{1,0:T(8,128)(2,1)S(1)}, u32[]{:S(2)}, u32[]{:S(2)}) %collective-permute-start.15) | collective-permute-done | bytes 262176 | tf_op jit(solution)/shard_map/ppermute | solution.py:24
  130.6 4.4 %collective-permute-done.16 = bf16[48,1024]{1,0:T(8,128)(2,1)S(1)} collective-permute-done((bf16[48,1024]{1,0:T(8,128)(2,1)S(1)}, bf16[48,1024]{1,0:T(8,128)(2,1)S(1)}, u32[]{:S(2)}, u32[]{:S(2)}) %collective-permute-start.16) | collective-permute-done | bytes 98336 | tf_op jit(solution)/shard_map/ppermute | solution.py:24
  136.4 5.1 %collective-permute-start.23 = (bf16[96,1024]{1,0:T(8,128)(2,1)S(1)}, bf16[96,1024]{1,0:T(8,128)(2,1)S(1)}, u32[]{:S(2)}, u32[]{:S(2)}) collective-permute-start(bf16[96,1024]{1,0:T(8,128)(2,1)S(1)} %pad_maximum_fusion.4.refs_10_), channel_id=1, source_target_pairs={{0,24},{1,25},{2,26},{3,27},{4,28},{5,29},{6,30},{7,31},{8,0},{9,1... | collective-permute-start | bytes 589832 | tf_op jit(solution)/shard_map/ppermute | solution.py:33
  142.7 10.7 %shard_map.61.refs_14_ = bf16[256,8192]{1,0:T(8,128)(2,1)} custom-call(s32[2]{0:T(128)} %iota_add_fusion.group_ref, s32[1024]{0:T(1024)} %reshape.25.list_ref, s32[128]{0:T(128)} %reshape.26.count_ref, s32[1]{0:T(128)} %bitcast.me_ref, bf16[256,8192]{1,0:T(8,128)(2,1)} %bitcast.10, bf16[256,512]{1,0:T(8,128)(2,1)} %copy-done.2, ...), custom_call_target="tpu_custom_call", output_to_operand_aliasing={{}: (10, {})} | custom-call | flops 1 | bytes 1 | tf_op jit(solution)/shard_map/pallas_call | solution.py:282
  155.2 20.2 %shard_map.62 = bf16[256,8192]{1,0:T(8,128)(2,1)} custom-call(s32[4]{0:T(128)} %pad_add_fusion.group_ref, s32[1024]{0:T(1024)} %reshape.25.list_ref, s32[128]{0:T(128)} %reshape.26.count_ref, s32[1]{0:T(128)} %bitcast.me_ref, bf16[256,8192]{1,0:T(8,128)(2,1)} %bitcast.11, bf16[128,1024]{1,0:T(8,128)(2,1)} %copy-done.8, ...), custom_call_target="tpu_custom_call", output_to_operand_aliasing={{}: (19, {})} | custom-call | flops 1 | bytes 1 | tf_op jit(solution)/shard_map/pallas_call | solution.py:282
  (92 shorter events, 16.0 us)
Async XLA Ops:
  0.0 16.0 %collective-permute-start.1 = (bf16[8192,512]{1,0:T(8,128)(2,1)}, bf16[8192,512]{1,0:T(8,128)(2,1)}, u32[]{:S(2)}, u32[]{:S(2)}) collective-permute-start(bf16[8192,512]{1,0:T(8,128)(2,1)} %refs_0_.5), channel_id=1, source_target_pairs={{0,1},{1,0},{2,3},{3,2},{4,5},{5,4},{6,7},{7,6},{8,9},{9,8},{10,11... | collective-permute-start | bytes 25165832 | tf_op jit(solution)/shard_map/ppermute | solution.py:24
  2.8 48.9 %collective-permute-start = (bf16[128,8192]{1,0:T(8,128)(2,1)S(1)}, bf16[128,8192]{1,0:T(8,128)(2,1)S(1)}, u32[]{:S(2)}, u32[]{:S(2)}) collective-permute-start(bf16[128,8192]{1,0:T(8,128)(2,1)S(1)} %shard_map.55), channel_id=1, source_target_pairs={{0,2},{1,3},{2,0},{3,1},{4,6},{5,7},{6,4},{7,5},{8,10},{9,11},{10,... | collective-permute-start | bytes 6291464 | tf_op jit(solution)/shard_map/ppermute | solution.py:24
  10.9 15.9 %collective-permute-start.4 = (bf16[256,512]{1,0:T(8,128)(2,1)S(1)}, bf16[256,512]{1,0:T(8,128)(2,1)S(1)}, u32[]{:S(2)}, u32[]{:S(2)}) collective-permute-start(bf16[256,512]{1,0:T(8,128)(2,1)S(1)} %shard_map.56.refs_0_), channel_id=1, source_target_pairs={{0,16},{1,17},{2,18},{3,19},{4,20},{5,21},{6,22},{7,23},{8,24},{9,... | collective-permute-start | bytes 786440 | tf_op jit(solution)/shard_map/ppermute | solution.py:33
  14.0 12.9 %collective-permute-start.3 = (bf16[256,512]{1,0:T(8,128)(2,1)S(1)}, bf16[256,512]{1,0:T(8,128)(2,1)S(1)}, u32[]{:S(2)}, u32[]{:S(2)}) collective-permute-start(bf16[256,512]{1,0:T(8,128)(2,1)S(1)} %shard_map.56.refs_0_), channel_id=1, source_target_pairs={{0,24},{1,25},{2,26},{3,27},{4,28},{5,29},{6,30},{7,31},{8,0},{9,1... | collective-permute-start | bytes 786440 | tf_op jit(solution)/shard_map/ppermute | solution.py:33
  15.3 18.1 %collective-permute-start.2 = (bf16[256,512]{1,0:T(8,128)(2,1)S(1)}, bf16[256,512]{1,0:T(8,128)(2,1)S(1)}, u32[]{:S(2)}, u32[]{:S(2)}) collective-permute-start(bf16[256,512]{1,0:T(8,128)(2,1)S(1)} %shard_map.56.refs_0_), channel_id=1, source_target_pairs={{0,8},{1,9},{2,10},{3,11},{4,12},{5,13},{6,14},{7,15},{8,16},{9,17... | collective-permute-start | bytes 786440 | tf_op jit(solution)/shard_map/ppermute | solution.py:33
  20.0 45.0 %copy-start.2 = (bf16[256,512]{1,0:T(8,128)(2,1)}, bf16[256,512]{1,0:T(8,128)(2,1)S(1)}, u32[]{:S(2)}) copy-start(bf16[256,512]{1,0:T(8,128)(2,1)S(1)} %shard_map.57.refs_0_) | copy-start | bytes 786436
  26.8 38.1 %copy-start.12 = (bf16[256,512]{1,0:T(8,128)(2,1)}, bf16[256,512]{1,0:T(8,128)(2,1)S(1)}, u32[]{:S(2)}) copy-start(bf16[256,512]{1,0:T(8,128)(2,1)S(1)} %collective-permute-done.4.refs_3_) | copy-start | bytes 786436
  26.9 38.1 %copy-start.13 = (bf16[256,512]{1,0:T(8,128)(2,1)}, bf16[256,512]{1,0:T(8,128)(2,1)S(1)}, u32[]{:S(2)}) copy-start(bf16[256,512]{1,0:T(8,128)(2,1)S(1)} %collective-permute-done.3.refs_2_) | copy-start | bytes 786436
  33.4 31.5 %copy-start.14 = (bf16[256,512]{1,0:T(8,128)(2,1)}, bf16[256,512]{1,0:T(8,128)(2,1)S(1)}, u32[]{:S(2)}) copy-start(bf16[256,512]{1,0:T(8,128)(2,1)S(1)} %collective-permute-done.2.refs_1_) | copy-start | bytes 786436
  33.5 24.8 %collective-permute-start.5 = (bf16[1024,512]{1,0:T(8,128)(2,1)S(1)}, bf16[1024,512]{1,0:T(8,128)(2,1)S(1)}, u32[]{:S(2)}, u32[]{:S(2)}) collective-permute-start(bf16[1024,512]{1,0:T(8,128)(2,1)S(1)} %pad_maximum_fusion), channel_id=1, source_target_pairs={{0,4},{4,0},{8,12},{12,8},{16,20},{20,16},{24,28},{28,24},{1,5},{5... | collective-permute-start | bytes 3145736 | tf_op jit(solution)/shard_map/ppermute | solution.py:24
  35.1 30.0 %collective-permute-start.8 = (bf16[256,512]{1,0:T(8,128)(2,1)S(1)}, bf16[256,512]{1,0:T(8,128)(2,1)S(1)}, u32[]{:S(2)}, u32[]{:S(2)}) collective-permute-start(bf16[256,512]{1,0:T(8,128)(2,1)S(1)} %shard_map.57.refs_0_), channel_id=1, source_target_pairs={{0,16},{1,17},{2,18},{3,19},{4,20},{5,21},{6,22},{7,23},{8,24},{9,... | collective-permute-start | bytes 786440 | tf_op jit(solution)/shard_map/ppermute | solution.py:33
  42.1 22.9 %collective-permute-start.7 = (bf16[256,512]{1,0:T(8,128)(2,1)S(1)}, bf16[256,512]{1,0:T(8,128)(2,1)S(1)}, u32[]{:S(2)}, u32[]{:S(2)}) collective-permute-start(bf16[256,512]{1,0:T(8,128)(2,1)S(1)} %shard_map.57.refs_0_), channel_id=1, source_target_pairs={{0,24},{1,25},{2,26},{3,27},{4,28},{5,29},{6,30},{7,31},{8,0},{9,1... | collective-permute-start | bytes 786440 | tf_op jit(solution)/shard_map/ppermute | solution.py:33
  42.6 22.4 %collective-permute-start.6 = (bf16[256,512]{1,0:T(8,128)(2,1)S(1)}, bf16[256,512]{1,0:T(8,128)(2,1)S(1)}, u32[]{:S(2)}, u32[]{:S(2)}) collective-permute-start(bf16[256,512]{1,0:T(8,128)(2,1)S(1)} %shard_map.57.refs_0_), channel_id=1, source_target_pairs={{0,8},{1,9},{2,10},{3,11},{4,12},{5,13},{6,14},{7,15},{8,16},{9,17... | collective-permute-start | bytes 786440 | tf_op jit(solution)/shard_map/ppermute | solution.py:33
  51.7 53.3 %collective-permute-start.14 = (bf16[128,8192]{1,0:T(8,128)(2,1)}, bf16[128,8192]{1,0:T(8,128)(2,1)S(1)}, u32[]{:S(2)}, u32[]{:S(2)}) collective-permute-start(bf16[128,8192]{1,0:T(8,128)(2,1)} %slice_bitcast_fusion), channel_id=1, source_target_pairs={{0,2},{1,3},{2,0},{3,1},{4,6},{5,7},{6,4},{7,5},{8,10},{9,11},{10,... | collective-permute-start | bytes 6291464 | tf_op jit(solution)/shard_map/ppermute | solution.py:24
  65.0 31.5 %copy-start.5 = (bf16[256,512]{1,0:T(8,128)(2,1)}, bf16[256,512]{1,0:T(8,128)(2,1)S(1)}, u32[]{:S(2)}) copy-start(bf16[256,512]{1,0:T(8,128)(2,1)S(1)} %collective-permute-done.8.refs_3_) | copy-start | bytes 786436
  65.0 31.4 %copy-start.6 = (bf16[256,512]{1,0:T(8,128)(2,1)}, bf16[256,512]{1,0:T(8,128)(2,1)S(1)}, u32[]{:S(2)}) copy-start(bf16[256,512]{1,0:T(8,128)(2,1)S(1)} %collective-permute-done.7.refs_2_) | copy-start | bytes 786436
  65.1 31.4 %copy-start.7 = (bf16[256,512]{1,0:T(8,128)(2,1)}, bf16[256,512]{1,0:T(8,128)(2,1)S(1)}, u32[]{:S(2)}) copy-start(bf16[256,512]{1,0:T(8,128)(2,1)S(1)} %collective-permute-done.6.refs_1_) | copy-start | bytes 786436
  66.2 34.1 %collective-permute-start.10 = (bf16[1024,512]{1,0:T(8,128)(2,1)}, bf16[1024,512]{1,0:T(8,128)(2,1)}, u32[]{:S(2)}, u32[]{:S(2)}) collective-permute-start(bf16[1024,512]{1,0:T(8,128)(2,1)} %pad_maximum_fusion.1), channel_id=1, source_target_pairs={{0,4},{4,0},{8,12},{12,8},{16,20},{20,16},{24,28},{28,24},{1,5},{5... | collective-permute-start | bytes 3145736 | tf_op jit(solution)/shard_map/ppermute | solution.py:24
  67.7 11.2 %collective-permute-start.9 = (bf16[128,1024]{1,0:T(8,128)(2,1)S(1)}, bf16[128,1024]{1,0:T(8,128)(2,1)S(1)}, u32[]{:S(2)}, u32[]{:S(2)}) collective-permute-start(bf16[128,1024]{1,0:T(8,128)(2,1)S(1)} %shard_map.58), channel_id=1, source_target_pairs={{0,10},{1,11},{2,8},{3,9},{4,14},{5,15},{6,12},{7,13},{8,18},{9,19... | collective-permute-start | bytes 786440 | tf_op jit(solution)/shard_map/ppermute | solution.py:33
  78.9 20.5 %collective-permute-start.13 = (bf16[128,1024]{1,0:T(8,128)(2,1)S(1)}, bf16[128,1024]{1,0:T(8,128)(2,1)S(1)}, u32[]{:S(2)}, u32[]{:S(2)}) collective-permute-start(bf16[128,1024]{1,0:T(8,128)(2,1)S(1)} %collective-permute-done.9.refs_0_), channel_id=1, source_target_pairs={{0,16},{1,17},{2,18},{3,19},{4,20},{5,21},{6,22},{7,23},{8,24},{9,... | collective-permute-start | bytes 786440 | tf_op jit(solution)/shard_map/ppermute | solution.py:33
  83.4 17.0 %collective-permute-start.12 = (bf16[128,1024]{1,0:T(8,128)(2,1)S(1)}, bf16[128,1024]{1,0:T(8,128)(2,1)}, u32[]{:S(2)}, u32[]{:S(2)}) collective-permute-start(bf16[128,1024]{1,0:T(8,128)(2,1)S(1)} %collective-permute-done.9.refs_0_), channel_id=1, source_target_pairs={{0,24},{1,25},{2,26},{3,27},{4,28},{5,29},{6,30},{7,31},{8,0},{9,1... | collective-permute-start | bytes 786440 | tf_op jit(solution)/shard_map/ppermute | solution.py:33
  83.8 16.5 %collective-permute-start.11 = (bf16[128,1024]{1,0:T(8,128)(2,1)S(1)}, bf16[128,1024]{1,0:T(8,128)(2,1)}, u32[]{:S(2)}, u32[]{:S(2)}) collective-permute-start(bf16[128,1024]{1,0:T(8,128)(2,1)S(1)} %collective-permute-done.9.refs_0_), channel_id=1, source_target_pairs={{0,8},{1,9},{2,10},{3,11},{4,12},{5,13},{6,14},{7,15},{8,16},{9,17... | collective-permute-start | bytes 786440 | tf_op jit(solution)/shard_map/ppermute | solution.py:33
  101.5 33.5 %collective-permute-start.17 = (bf16[512,1024]{1,0:T(8,128)(2,1)S(1)}, bf16[512,1024]{1,0:T(8,128)(2,1)S(1)}, u32[]{:S(2)}, u32[]{:S(2)}) collective-permute-start(bf16[512,1024]{1,0:T(8,128)(2,1)S(1)} %pad_maximum_fusion.2), channel_id=1, source_target_pairs={{0,4},{4,0},{8,12},{12,8},{16,20},{20,16},{24,28},{28,24},{1,5},{5... | collective-permute-start | bytes 3145736 | tf_op jit(solution)/shard_map/ppermute | solution.py:24
  111.3 17.9 %collective-permute-start.15 = (bf16[128,1024]{1,0:T(8,128)(2,1)S(1)}, bf16[128,1024]{1,0:T(8,128)(2,1)S(1)}, u32[]{:S(2)}, u32[]{:S(2)}) collective-permute-start(bf16[128,1024]{1,0:T(8,128)(2,1)S(1)} %shard_map.60), channel_id=1, source_target_pairs={{0,2},{1,3},{2,0},{3,1},{4,6},{5,7},{6,4},{7,5},{8,10},{9,11},{10,... | collective-permute-start | bytes 786440 | tf_op jit(solution)/shard_map/ppermute | solution.py:24
  112.9 17.6 %collective-permute-start.20 = (bf16[80,1024]{1,0:T(8,128)(2,1)S(1)}, bf16[80,1024]{1,0:T(8,128)(2,1)S(1)}, u32[]{:S(2)}, u32[]{:S(2)}) collective-permute-start(bf16[80,1024]{1,0:T(8,128)(2,1)S(1)} %slice.25), channel_id=1, source_target_pairs={{0,18},{1,19},{2,16},{3,17},{4,22},{5,23},{6,20},{7,21},{8,26},{9,... | collective-permute-start | bytes 491528 | tf_op jit(solution)/shard_map/ppermute | solution.py:33
  116.2 14.3 %collective-permute-start.19 = (bf16[80,1024]{1,0:T(8,128)(2,1)S(1)}, bf16[80,1024]{1,0:T(8,128)(2,1)S(1)}, u32[]{:S(2)}, u32[]{:S(2)}) collective-permute-start(bf16[80,1024]{1,0:T(8,128)(2,1)S(1)} %slice.25), channel_id=1, source_target_pairs={{0,26},{1,27},{2,24},{3,25},{4,30},{5,31},{6,28},{7,29},{8,2},{9,3... | collective-permute-start | bytes 491528 | tf_op jit(solution)/shard_map/ppermute | solution.py:33
  118.3 12.2 %collective-permute-start.18 = (bf16[80,1024]{1,0:T(8,128)(2,1)S(1)}, bf16[80,1024]{1,0:T(8,128)(2,1)S(1)}, u32[]{:S(2)}, u32[]{:S(2)}) collective-permute-start(bf16[80,1024]{1,0:T(8,128)(2,1)S(1)} %slice.25), channel_id=1, source_target_pairs={{0,10},{1,11},{2,8},{3,9},{4,14},{5,15},{6,12},{7,13},{8,18},{9,19... | collective-permute-start | bytes 491528 | tf_op jit(solution)/shard_map/ppermute | solution.py:33
  129.1 5.8 %collective-permute-start.16 = (bf16[48,1024]{1,0:T(8,128)(2,1)S(1)}, bf16[48,1024]{1,0:T(8,128)(2,1)S(1)}, u32[]{:S(2)}, u32[]{:S(2)}) collective-permute-start(bf16[48,1024]{1,0:T(8,128)(2,1)S(1)} %slice.24), channel_id=1, source_target_pairs={{0,4},{4,0},{8,12},{12,8},{16,20},{20,16},{24,28},{28,24},{1,5},{5... | collective-permute-start | bytes 294920 | tf_op jit(solution)/shard_map/ppermute | solution.py:24
  135.0 18.6 %collective-permute-start.21 = (bf16[320,1024]{1,0:T(8,128)(2,1)S(1)}, bf16[320,1024]{1,0:T(8,128)(2,1)S(1)}, u32[]{:S(2)}, u32[]{:S(2)}) collective-permute-start(bf16[320,1024]{1,0:T(8,128)(2,1)S(1)} %pad_maximum_fusion.3), channel_id=1, source_target_pairs={{0,4},{4,0},{8,12},{12,8},{16,20},{20,16},{24,28},{28,24},{1,5},{5... | collective-permute-start | bytes 1966088 | tf_op jit(solution)/shard_map/ppermute | solution.py:24
  136.4 17.1 %collective-permute-start.24 = (bf16[96,1024]{1,0:T(8,128)(2,1)S(1)}, bf16[96,1024]{1,0:T(8,128)(2,1)S(1)}, u32[]{:S(2)}, u32[]{:S(2)}) collective-permute-start(bf16[96,1024]{1,0:T(8,128)(2,1)S(1)} %pad_maximum_fusion.4.refs_10_), channel_id=1, source_target_pairs={{0,16},{1,17},{2,18},{3,19},{4,20},{5,21},{6,22},{7,23},{8,24},{9,... | collective-permute-start | bytes 589832 | tf_op jit(solution)/shard_map/ppermute | solution.py:33
  136.4 17.1 %collective-permute-start.23 = (bf16[96,1024]{1,0:T(8,128)(2,1)S(1)}, bf16[96,1024]{1,0:T(8,128)(2,1)S(1)}, u32[]{:S(2)}, u32[]{:S(2)}) collective-permute-start(bf16[96,1024]{1,0:T(8,128)(2,1)S(1)} %pad_maximum_fusion.4.refs_10_), channel_id=1, source_target_pairs={{0,24},{1,25},{2,26},{3,27},{4,28},{5,29},{6,30},{7,31},{8,0},{9,1... | collective-permute-start | bytes 589832 | tf_op jit(solution)/shard_map/ppermute | solution.py:33
  141.5 12.0 %collective-permute-start.22 = (bf16[96,1024]{1,0:T(8,128)(2,1)S(1)}, bf16[96,1024]{1,0:T(8,128)(2,1)S(1)}, u32[]{:S(2)}, u32[]{:S(2)}) collective-permute-start(bf16[96,1024]{1,0:T(8,128)(2,1)S(1)} %pad_maximum_fusion.4.refs_10_), channel_id=1, source_target_pairs={{0,8},{1,9},{2,10},{3,11},{4,12},{5,13},{6,14},{7,15},{8,16},{9,17... | collective-permute-start | bytes 589832 | tf_op jit(solution)/shard_map/ppermute | solution.py:33
  (18 other events, 239.3 us)
where the time goes:
time: 176 us
  Pallas kernels  61 us (35%)
  waiting for transfers between devices  51.6 us (29%)
  starting transfers between devices  51.4 us (29%)
  local copies, waits for them, and re-layouts  6.86 us (4%)
  other arithmetic  4.05 us (2%)
    pallas_call x3, Pallas kernels, attend(): pl.pallas_call(functools.partial(attend_kernel, places, (blocks, max_live...  40 us
    ppermute x16, starting transfers between devices, rotate(): return lax.ppermute(array, ('ctx', 'fsdp'), order)  38.7 us
    ppermute x9, waiting for transfers between devices, swap(): return lax.ppermute(array, axis, [(i, i ^ bit) for i in range(size)])  29.7 us
    ppermute x16, waiting for transfers between devices, rotate(): return lax.ppermute(array, ('ctx', 'fsdp'), order)  22 us
    pallas_call x4, Pallas kernels, project(): pl.pallas_call(functools.partial(project_kernel, n_weights, tile), out_sh...  20.9 us
    ppermute x9, starting transfers between devices, swap(): return lax.ppermute(array, axis, [(i, i ^ bit) for i in range(size)])  12.7 us
    unnamed x51, local copies, waits for them, and re-layouts  3.97 us
  transfers between devices with their start and end apart: 25, of which 11 were waited for; matrix products, arithmetic and copies ran while one was open for 4% of the time, Pallas kernels for 23%

commit v1 on v0

--- a/solution.py
+++ b/solution.py
@@ -342,13 +342,13 @@
     own_crossed = cross(jnp.concatenate(own_line, axis=0))
     near_turned = turn_all(near)
     second_got = swap(second_out, "fsdp", 2)
-    mark, first_got, own_crossed = pin(mark, first_got, own_crossed)
+    mark, first_got = pin(mark, first_got)
 
     def side_pieces(pieces, crossed):
         return line(pieces, [0, *steps], whole, 0) + [(crossed, [(r, 1, *whole) for r in [0, *steps]])]
 
     first = project(first_got, (kv_weight, near_weight))
-    mark, first, *near_turned = pin(mark, first, *near_turned)
+    mark, first, own_crossed, *near_turned = pin(mark, first, own_crossed, *near_turned)
     first = rotate(first, 1, 2)
     near_line = [near, *near_turned]
     near_crossed = cross(jnp.concatenate(near_line, axis=0))

time: 176 us -> 175 us (level)
  starting transfers between devices: 51.4 us -> 47.6 us
  Pallas kernels: 61 us -> 63.1 us
    ppermute x16, starting transfers between devices: 38.7 us -> 34.8 us  [rotate(): return lax.ppermute(array, ('ctx', 'fsdp'), order)]
    pallas_call x3, Pallas kernels: 40 us -> 42.5 us  [attend(): pl.pallas_call(functools.partial(attend_kernel, places, (blocks, max_live...]
  transfers between devices with their start and end apart: 25 -> 25, of which waited for: 11 -> 11; matrix products, arithmetic and copies ran while one was open for 4% -> 4% of each run, Pallas kernels for 23% -> 25%
where the time goes in v1:
time: 175 us
  Pallas kernels  63.1 us (36%)
  waiting for transfers between devices  53.3 us (30%)
  starting transfers between devices  47.6 us (27%)
  local copies, waits for them, and re-layouts  6.85 us (4%)
  other arithmetic  4.07 us (2%)
    pallas_call x3, Pallas kernels, attend(): pl.pallas_call(functools.partial(attend_kernel, places, (blocks, max_live...  42.5 us
    ppermute x16, starting transfers between devices, rotate(): return lax.ppermute(array, ('ctx', 'fsdp'), order)  34.8 us
    ppermute x9, waiting for transfers between devices, swap(): return lax.ppermute(array, axis, [(i, i ^ bit) for i in range(size)])  29.8 us
    ppermute x16, waiting for transfers between devices, rotate(): return lax.ppermute(array, ('ctx', 'fsdp'), order)  23.5 us
    pallas_call x4, Pallas kernels, project(): pl.pallas_call(functools.partial(project_kernel, n_weights, tile), out_sh...  20.5 us
    ppermute x9, starting transfers between devices, swap(): return lax.ppermute(array, axis, [(i, i ^ bit) for i in range(size)])  12.7 us
    unnamed x51, local copies, waits for them, and re-layouts  3.95 us
  transfers between devices with their start and end apart: 25, of which 11 were waited for; matrix products, arithmetic and copies ran while one was open for 4% of the time, Pallas kernels for 25%

profile of v1, /device:TPU:0, one launch (start us, length us, event | category | flops | bytes accessed | tf_op | source)
XLA Modules:
  0.0 175.5 jit_solution(3201049224094415826)
XLA Ops:
  0.5 2.2 %copy-done = bf16[1,256,8192]{2,1,0:T(8,128)(2,1)S(1)} copy-done((bf16[1,256,8192]{2,1,0:T(8,128)(2,1)S(1)}, bf16[1,256,8192]{2,1,0:T(8,128)(2,1)}, u32[]{:S(2)}) %copy-start) | copy-done | bytes 4194328
  2.8 2.6 %collective-permute-start = (bf16[128,8192]{1,0:T(8,128)(2,1)S(1)}, bf16[128,8192]{1,0:T(8,128)(2,1)S(1)}, u32[]{:S(2)}, u32[]{:S(2)}) collective-permute-start(bf16[128,8192]{1,0:T(8,128)(2,1)S(1)} %shard_map.55), channel_id=1, source_target_pairs={{0,2},{1,3},{2,0},{3,1},{4,6},{5,7},{6,4},{7,5},{8,10},{9,11},{10,... | collective-permute-start | bytes 6291464 | tf_op jit(solution)/shard_map/ppermute | solution.py:24
  5.4 1.5 slice_bitcast_fusion
  6.9 4.0 %shard_map.57.refs_0_ = bf16[256,512]{1,0:T(8,128)(2,1)S(1)} custom-call(bf16[256,8192]{1,0:T(8,128)(2,1)S(1)} %bitcast.7, bf16[8192,512]{1,0:T(8,128)(2,1)} %refs_0_.5), custom_call_target="tpu_custom_call" | custom-call | flops 1 | bytes 1 | tf_op jit(solution)/shard_map/pallas_call | solution.py:112
  10.9 3.1 %collective-permute-start.4 = (bf16[256,512]{1,0:T(8,128)(2,1)S(1)}, bf16[256,512]{1,0:T(8,128)(2,1)S(1)}, u32[]{:S(2)}, u32[]{:S(2)}) collective-permute-start(bf16[256,512]{1,0:T(8,128)(2,1)S(1)} %shard_map.57.refs_0_), channel_id=1, source_target_pairs={{0,16},{1,17},{2,18},{3,19},{4,20},{5,21},{6,22},{7,23},{8,24},{9,... | collective-permute-start | bytes 786440 | tf_op jit(solution)/shard_map/ppermute | solution.py:33
  16.0 4.0 %shard_map.58.refs_0_ = bf16[256,512]{1,0:T(8,128)(2,1)S(1)} custom-call(bf16[256,8192]{1,0:T(8,128)(2,1)S(1)} %bitcast.8, bf16[8192,512]{1,0:T(8,128)(2,1)} %collective-permute-done.1.refs_1_.refs_0_), custom_call_target="tpu_custom_call" | custom-call | flops 1 | bytes 1 | tf_op jit(solution)/shard_map/pallas_call | solution.py:112
  20.0 6.8 %collective-permute-done.4.refs_3_ = bf16[256,512]{1,0:T(8,128)(2,1)S(1)} collective-permute-done((bf16[256,512]{1,0:T(8,128)(2,1)S(1)}, bf16[256,512]{1,0:T(8,128)(2,1)S(1)}, u32[]{:S(2)}, u32[]{:S(2)}) %collective-permute-start.4) | collective-permute-done | bytes 262176 | tf_op jit(solution)/shard_map/ppermute | solution.py:33
  26.9 6.5 %collective-permute-done.2.refs_1_ = bf16[256,512]{1,0:T(8,128)(2,1)S(1)} collective-permute-done((bf16[256,512]{1,0:T(8,128)(2,1)S(1)}, bf16[256,512]{1,0:T(8,128)(2,1)S(1)}, u32[]{:S(2)}, u32[]{:S(2)}) %collective-permute-start.2) | collective-permute-done | bytes 262176 | tf_op jit(solution)/shard_map/ppermute | solution.py:33
  33.5 1.6 collective-permute-start.5
  35.1 7.1 %collective-permute-start.8 = (bf16[256,512]{1,0:T(8,128)(2,1)S(1)}, bf16[256,512]{1,0:T(8,128)(2,1)S(1)}, u32[]{:S(2)}, u32[]{:S(2)}) collective-permute-start(bf16[256,512]{1,0:T(8,128)(2,1)S(1)} %shard_map.58.refs_0_), channel_id=1, source_target_pairs={{0,16},{1,17},{2,18},{3,19},{4,20},{5,21},{6,22},{7,23},{8,24},{9,... | collective-permute-start | bytes 786440 | tf_op jit(solution)/shard_map/ppermute | solution.py:33
  42.6 1.6 collective-permute-start.6
  44.2 7.5 %collective-permute-done.row_ref = bf16[128,8192]{1,0:T(8,128)(2,1)S(1)} collective-permute-done((bf16[128,8192]{1,0:T(8,128)(2,1)S(1)}, bf16[128,8192]{1,0:T(8,128)(2,1)S(1)}, u32[]{:S(2)}, u32[]{:S(2)}) %collective-permute-start) | collective-permute-done | bytes 2097184 | tf_op jit(solution)/shard_map/ppermute | solution.py:24
  51.7 1.7 collective-permute-start.14
  53.4 6.3 %shard_map.56 = bf16[128,1024]{1,0:T(8,128)(2,1)S(1)} custom-call(bf16[128,8192]{1,0:T(8,128)(2,1)S(1)} %collective-permute-done.row_ref, bf16[8192,512]{1,0:T(8,128)(2,1)} %refs_0_.5, bf16[8192,512]{1,0:T(8,128)(2,1)} %collective-permute-done.1.refs_1_.refs_0_), custom_call_target="tpu_custom_call" | custom-call | flops 1 | bytes 1 | tf_op jit(solution)/shard_map/pallas_call | solution.py:112
  62.6 6.0 %collective-permute-start.9 = (bf16[128,1024]{1,0:T(8,128)(2,1)S(1)}, bf16[128,1024]{1,0:T(8,128)(2,1)S(1)}, u32[]{:S(2)}, u32[]{:S(2)}) collective-permute-start(bf16[128,1024]{1,0:T(8,128)(2,1)S(1)} %shard_map.56), channel_id=1, source_target_pairs={{0,10},{1,11},{2,8},{3,9},{4,14},{5,15},{6,12},{7,13},{8,18},{9,19... | collective-permute-start | bytes 786440 | tf_op jit(solution)/shard_map/ppermute | solution.py:33
  68.6 5.3 %collective-permute-done.9.refs_0_ = bf16[128,1024]{1,0:T(8,128)(2,1)S(1)} collective-permute-done((bf16[128,1024]{1,0:T(8,128)(2,1)S(1)}, bf16[128,1024]{1,0:T(8,128)(2,1)S(1)}, u32[]{:S(2)}, u32[]{:S(2)}) %collective-permute-start.9) | collective-permute-done | bytes 262176 | tf_op jit(solution)/shard_map/ppermute | solution.py:33
  74.0 2.7 %collective-permute-start.13 = (bf16[128,1024]{1,0:T(8,128)(2,1)S(1)}, bf16[128,1024]{1,0:T(8,128)(2,1)S(1)}, u32[]{:S(2)}, u32[]{:S(2)}) collective-permute-start(bf16[128,1024]{1,0:T(8,128)(2,1)S(1)} %collective-permute-done.9.refs_0_), channel_id=1, source_target_pairs={{0,16},{1,17},{2,18},{3,19},{4,20},{5,21},{6,22},{7,23},{8,24},{9,... | collective-permute-start | bytes 786440 | tf_op jit(solution)/shard_map/ppermute | solution.py:33
  76.7 2.1 %collective-permute-start.12 = (bf16[128,1024]{1,0:T(8,128)(2,1)S(1)}, bf16[128,1024]{1,0:T(8,128)(2,1)}, u32[]{:S(2)}, u32[]{:S(2)}) collective-permute-start(bf16[128,1024]{1,0:T(8,128)(2,1)S(1)} %collective-permute-done.9.refs_0_), channel_id=1, source_target_pairs={{0,24},{1,25},{2,26},{3,27},{4,28},{5,29},{6,30},{7,31},{8,0},{9,1... | collective-permute-start | bytes 786440 | tf_op jit(solution)/shard_map/ppermute | solution.py:33
  80.8 10.7 %shard_map.59.refs_5_ = bf16[256,8192]{1,0:T(8,128)(2,1)} custom-call(s32[2]{0:T(128)} %iota_add_fusion.1.group_ref, s32[1024]{0:T(1024)} %reshape.25.list_ref, s32[128]{0:T(128)} %reshape.26.count_ref, s32[1]{0:T(128)} %bitcast.me_ref, bf16[256,8192]{1,0:T(8,128)(2,1)} %bitcast.9, bf16[256,512]{1,0:T(8,128)(2,1)} %copy-done.3, bf16[256,512]{1,0:T(8,128)(2,1)} %copy-done.14, ...), custom_call_target="tpu_custom_call" | custom-call | flops 1 | bytes 1 | tf_op jit(solution)/shard_map/pallas_call | solution.py:282
  91.5 3.6 %collective-permute-done.13.refs_3_ = bf16[128,1024]{1,0:T(8,128)(2,1)S(1)} collective-permute-done((bf16[128,1024]{1,0:T(8,128)(2,1)S(1)}, bf16[128,1024]{1,0:T(8,128)(2,1)S(1)}, u32[]{:S(2)}, u32[]{:S(2)}) %collective-permute-start.13) | collective-permute-done | bytes 262176 | tf_op jit(solution)/shard_map/ppermute | solution.py:33
  96.2 1.6 collective-permute-start.17
  97.8 7.2 %collective-permute-done.14.row_ref = bf16[128,8192]{1,0:T(8,128)(2,1)S(1)} collective-permute-done((bf16[128,8192]{1,0:T(8,128)(2,1)}, bf16[128,8192]{1,0:T(8,128)(2,1)S(1)}, u32[]{:S(2)}, u32[]{:S(2)}) %collective-permute-start.14) | collective-permute-done | bytes 2097184 | tf_op jit(solution)/shard_map/ppermute | solution.py:24
  105.0 6.3 %shard_map.60 = bf16[128,1024]{1,0:T(8,128)(2,1)S(1)} custom-call(bf16[128,8192]{1,0:T(8,128)(2,1)S(1)} %collective-permute-done.14.row_ref, bf16[8192,512]{1,0:T(8,128)(2,1)} %refs_0_.5, bf16[8192,512]{1,0:T(8,128)(2,1)} %collective-permute-done.1.refs_1_.refs_0_), custom_call_target="tpu_custom_call" | custom-call | flops 1 | bytes 1 | tf_op jit(solution)/shard_map/pallas_call | solution.py:112
  111.3 1.6 collective-permute-start.15
  112.9 2.6 %collective-permute-start.20 = (bf16[80,1024]{1,0:T(8,128)(2,1)S(1)}, bf16[80,1024]{1,0:T(8,128)(2,1)S(1)}, u32[]{:S(2)}, u32[]{:S(2)}) collective-permute-start(bf16[80,1024]{1,0:T(8,128)(2,1)S(1)} %slice.25), channel_id=1, source_target_pairs={{0,18},{1,19},{2,16},{3,17},{4,22},{5,23},{6,20},{7,21},{8,26},{9,... | collective-permute-start | bytes 491528 | tf_op jit(solution)/shard_map/ppermute | solution.py:33
  115.5 2.3 %collective-permute-start.19 = (bf16[80,1024]{1,0:T(8,128)(2,1)S(1)}, bf16[80,1024]{1,0:T(8,128)(2,1)S(1)}, u32[]{:S(2)}, u32[]{:S(2)}) collective-permute-start(bf16[80,1024]{1,0:T(8,128)(2,1)S(1)} %slice.25), channel_id=1, source_target_pairs={{0,26},{1,27},{2,24},{3,25},{4,30},{5,31},{6,28},{7,29},{8,2},{9,3... | collective-permute-start | bytes 491528 | tf_op jit(solution)/shard_map/ppermute | solution.py:33
  118.4 10.7 %collective-permute-done.15 = bf16[128,1024]{1,0:T(8,128)(2,1)S(1)} collective-permute-done((bf16[128,1024]{1,0:T(8,128)(2,1)S(1)}, bf16[128,1024]{1,0:T(8,128)(2,1)S(1)}, u32[]{:S(2)}, u32[]{:S(2)}) %collective-permute-start.15) | collective-permute-done | bytes 262176 | tf_op jit(solution)/shard_map/ppermute | solution.py:24
  130.6 4.3 %collective-permute-done.16 = bf16[48,1024]{1,0:T(8,128)(2,1)S(1)} collective-permute-done((bf16[48,1024]{1,0:T(8,128)(2,1)S(1)}, bf16[48,1024]{1,0:T(8,128)(2,1)S(1)}, u32[]{:S(2)}, u32[]{:S(2)}) %collective-permute-start.16) | collective-permute-done | bytes 98336 | tf_op jit(solution)/shard_map/ppermute | solution.py:24
  135.0 1.4 collective-permute-start.21
  136.5 3.7 %collective-permute-start.23 = (bf16[96,1024]{1,0:T(8,128)(2,1)S(1)}, bf16[96,1024]{1,0:T(8,128)(2,1)S(1)}, u32[]{:S(2)}, u32[]{:S(2)}) collective-permute-start(bf16[96,1024]{1,0:T(8,128)(2,1)S(1)} %pad_maximum_fusion.4.refs_10_), channel_id=1, source_target_pairs={{0,24},{1,25},{2,26},{3,27},{4,28},{5,29},{6,30},{7,31},{8,0},{9,1... | collective-permute-start | bytes 589832 | tf_op jit(solution)/shard_map/ppermute | solution.py:33
  141.7 11.9 %shard_map.61.refs_14_ = bf16[256,8192]{1,0:T(8,128)(2,1)} custom-call(s32[2]{0:T(128)} %iota_add_fusion.group_ref, s32[1024]{0:T(1024)} %reshape.25.list_ref, s32[128]{0:T(128)} %reshape.26.count_ref, s32[1]{0:T(128)} %bitcast.me_ref, bf16[256,8192]{1,0:T(8,128)(2,1)} %bitcast.10, bf16[256,512]{1,0:T(8,128)(2,1)} %copy-done.2, ...), custom_call_target="tpu_custom_call", output_to_operand_aliasing={{}: (10, {})} | custom-call | flops 1 | bytes 1 | tf_op jit(solution)/shard_map/pallas_call | solution.py:282
  155.4 19.9 %shard_map.62 = bf16[256,8192]{1,0:T(8,128)(2,1)} custom-call(s32[4]{0:T(128)} %pad_add_fusion.group_ref, s32[1024]{0:T(1024)} %reshape.25.list_ref, s32[128]{0:T(128)} %reshape.26.count_ref, s32[1]{0:T(128)} %bitcast.me_ref, bf16[256,8192]{1,0:T(8,128)(2,1)} %bitcast.11, bf16[128,1024]{1,0:T(8,128)(2,1)} %copy-done.8, ...), custom_call_target="tpu_custom_call", output_to_operand_aliasing={{}: (19, {})} | custom-call | flops 1 | bytes 1 | tf_op jit(solution)/shard_map/pallas_call | solution.py:282
  (92 shorter events, 14.6 us)
Async XLA Ops:
  0.0 16.0 %collective-permute-start.1 = (bf16[8192,512]{1,0:T(8,128)(2,1)}, bf16[8192,512]{1,0:T(8,128)(2,1)}, u32[]{:S(2)}, u32[]{:S(2)}) collective-permute-start(bf16[8192,512]{1,0:T(8,128)(2,1)} %refs_0_.5), channel_id=1, source_target_pairs={{0,1},{1,0},{2,3},{3,2},{4,5},{5,4},{6,7},{7,6},{8,9},{9,8},{10,11... | collective-permute-start | bytes 25165832 | tf_op jit(solution)/shard_map/ppermute | solution.py:24
  2.8 48.9 %collective-permute-start = (bf16[128,8192]{1,0:T(8,128)(2,1)S(1)}, bf16[128,8192]{1,0:T(8,128)(2,1)S(1)}, u32[]{:S(2)}, u32[]{:S(2)}) collective-permute-start(bf16[128,8192]{1,0:T(8,128)(2,1)S(1)} %shard_map.55), channel_id=1, source_target_pairs={{0,2},{1,3},{2,0},{3,1},{4,6},{5,7},{6,4},{7,5},{8,10},{9,11},{10,... | collective-permute-start | bytes 6291464 | tf_op jit(solution)/shard_map/ppermute | solution.py:24
  10.9 15.9 %collective-permute-start.4 = (bf16[256,512]{1,0:T(8,128)(2,1)S(1)}, bf16[256,512]{1,0:T(8,128)(2,1)S(1)}, u32[]{:S(2)}, u32[]{:S(2)}) collective-permute-start(bf16[256,512]{1,0:T(8,128)(2,1)S(1)} %shard_map.57.refs_0_), channel_id=1, source_target_pairs={{0,16},{1,17},{2,18},{3,19},{4,20},{5,21},{6,22},{7,23},{8,24},{9,... | collective-permute-start | bytes 786440 | tf_op jit(solution)/shard_map/ppermute | solution.py:33
  14.0 12.9 %collective-permute-start.3 = (bf16[256,512]{1,0:T(8,128)(2,1)S(1)}, bf16[256,512]{1,0:T(8,128)(2,1)S(1)}, u32[]{:S(2)}, u32[]{:S(2)}) collective-permute-start(bf16[256,512]{1,0:T(8,128)(2,1)S(1)} %shard_map.57.refs_0_), channel_id=1, source_target_pairs={{0,24},{1,25},{2,26},{3,27},{4,28},{5,29},{6,30},{7,31},{8,0},{9,1... | collective-permute-start | bytes 786440 | tf_op jit(solution)/shard_map/ppermute | solution.py:33
  15.3 18.1 %collective-permute-start.2 = (bf16[256,512]{1,0:T(8,128)(2,1)S(1)}, bf16[256,512]{1,0:T(8,128)(2,1)S(1)}, u32[]{:S(2)}, u32[]{:S(2)}) collective-permute-start(bf16[256,512]{1,0:T(8,128)(2,1)S(1)} %shard_map.57.refs_0_), channel_id=1, source_target_pairs={{0,8},{1,9},{2,10},{3,11},{4,12},{5,13},{6,14},{7,15},{8,16},{9,17... | collective-permute-start | bytes 786440 | tf_op jit(solution)/shard_map/ppermute | solution.py:33
  20.0 40.8 %copy-start.2 = (bf16[256,512]{1,0:T(8,128)(2,1)}, bf16[256,512]{1,0:T(8,128)(2,1)S(1)}, u32[]{:S(2)}) copy-start(bf16[256,512]{1,0:T(8,128)(2,1)S(1)} %shard_map.58.refs_0_) | copy-start | bytes 786436
  26.8 32.9 %copy-start.12 = (bf16[256,512]{1,0:T(8,128)(2,1)}, bf16[256,512]{1,0:T(8,128)(2,1)S(1)}, u32[]{:S(2)}) copy-start(bf16[256,512]{1,0:T(8,128)(2,1)S(1)} %collective-permute-done.4.refs_3_) | copy-start | bytes 786436
  26.9 32.8 %copy-start.13 = (bf16[256,512]{1,0:T(8,128)(2,1)}, bf16[256,512]{1,0:T(8,128)(2,1)S(1)}, u32[]{:S(2)}) copy-start(bf16[256,512]{1,0:T(8,128)(2,1)S(1)} %collective-permute-done.3.refs_2_) | copy-start | bytes 786436
  33.4 26.3 %copy-start.14 = (bf16[256,512]{1,0:T(8,128)(2,1)}, bf16[256,512]{1,0:T(8,128)(2,1)S(1)}, u32[]{:S(2)}) copy-start(bf16[256,512]{1,0:T(8,128)(2,1)S(1)} %collective-permute-done.2.refs_1_) | copy-start | bytes 786436
  33.5 27.4 %collective-permute-start.5 = (bf16[1024,512]{1,0:T(8,128)(2,1)S(1)}, bf16[1024,512]{1,0:T(8,128)(2,1)S(1)}, u32[]{:S(2)}, u32[]{:S(2)}) collective-permute-start(bf16[1024,512]{1,0:T(8,128)(2,1)S(1)} %pad_maximum_fusion), channel_id=1, source_target_pairs={{0,4},{4,0},{8,12},{12,8},{16,20},{20,16},{24,28},{28,24},{1,5},{5... | collective-permute-start | bytes 3145736 | tf_op jit(solution)/shard_map/ppermute | solution.py:24
  35.1 24.7 %collective-permute-start.8 = (bf16[256,512]{1,0:T(8,128)(2,1)S(1)}, bf16[256,512]{1,0:T(8,128)(2,1)S(1)}, u32[]{:S(2)}, u32[]{:S(2)}) collective-permute-start(bf16[256,512]{1,0:T(8,128)(2,1)S(1)} %shard_map.58.refs_0_), channel_id=1, source_target_pairs={{0,16},{1,17},{2,18},{3,19},{4,20},{5,21},{6,22},{7,23},{8,24},{9,... | collective-permute-start | bytes 786440 | tf_op jit(solution)/shard_map/ppermute | solution.py:33
  42.1 18.7 %collective-permute-start.7 = (bf16[256,512]{1,0:T(8,128)(2,1)S(1)}, bf16[256,512]{1,0:T(8,128)(2,1)S(1)}, u32[]{:S(2)}, u32[]{:S(2)}) collective-permute-start(bf16[256,512]{1,0:T(8,128)(2,1)S(1)} %shard_map.58.refs_0_), channel_id=1, source_target_pairs={{0,24},{1,25},{2,26},{3,27},{4,28},{5,29},{6,30},{7,31},{8,0},{9,1... | collective-permute-start | bytes 786440 | tf_op jit(solution)/shard_map/ppermute | solution.py:33
  42.6 18.2 %collective-permute-start.6 = (bf16[256,512]{1,0:T(8,128)(2,1)S(1)}, bf16[256,512]{1,0:T(8,128)(2,1)S(1)}, u32[]{:S(2)}, u32[]{:S(2)}) collective-permute-start(bf16[256,512]{1,0:T(8,128)(2,1)S(1)} %shard_map.58.refs_0_), channel_id=1, source_target_pairs={{0,8},{1,9},{2,10},{3,11},{4,12},{5,13},{6,14},{7,15},{8,16},{9,17... | collective-permute-start | bytes 786440 | tf_op jit(solution)/shard_map/ppermute | solution.py:33
  51.7 53.3 %collective-permute-start.14 = (bf16[128,8192]{1,0:T(8,128)(2,1)}, bf16[128,8192]{1,0:T(8,128)(2,1)S(1)}, u32[]{:S(2)}, u32[]{:S(2)}) collective-permute-start(bf16[128,8192]{1,0:T(8,128)(2,1)} %slice_bitcast_fusion), channel_id=1, source_target_pairs={{0,2},{1,3},{2,0},{3,1},{4,6},{5,7},{6,4},{7,5},{8,10},{9,11},{10,... | collective-permute-start | bytes 6291464 | tf_op jit(solution)/shard_map/ppermute | solution.py:24
  59.8 31.7 %copy-start.5 = (bf16[256,512]{1,0:T(8,128)(2,1)}, bf16[256,512]{1,0:T(8,128)(2,1)S(1)}, u32[]{:S(2)}) copy-start(bf16[256,512]{1,0:T(8,128)(2,1)S(1)} %collective-permute-done.8.refs_3_) | copy-start | bytes 786436
  60.8 30.6 %copy-start.6 = (bf16[256,512]{1,0:T(8,128)(2,1)}, bf16[256,512]{1,0:T(8,128)(2,1)S(1)}, u32[]{:S(2)}) copy-start(bf16[256,512]{1,0:T(8,128)(2,1)S(1)} %collective-permute-done.7.refs_2_) | copy-start | bytes 786436
  60.8 30.6 %copy-start.7 = (bf16[256,512]{1,0:T(8,128)(2,1)}, bf16[256,512]{1,0:T(8,128)(2,1)S(1)}, u32[]{:S(2)}) copy-start(bf16[256,512]{1,0:T(8,128)(2,1)S(1)} %collective-permute-done.6.refs_1_) | copy-start | bytes 786436
  62.1 33.0 %collective-permute-start.10 = (bf16[1024,512]{1,0:T(8,128)(2,1)}, bf16[1024,512]{1,0:T(8,128)(2,1)}, u32[]{:S(2)}, u32[]{:S(2)}) collective-permute-start(bf16[1024,512]{1,0:T(8,128)(2,1)} %pad_maximum_fusion.1), channel_id=1, source_target_pairs={{0,4},{4,0},{8,12},{12,8},{16,20},{20,16},{24,28},{28,24},{1,5},{5... | collective-permute-start | bytes 3145736 | tf_op jit(solution)/shard_map/ppermute | solution.py:24
  62.6 11.3 %collective-permute-start.9 = (bf16[128,1024]{1,0:T(8,128)(2,1)S(1)}, bf16[128,1024]{1,0:T(8,128)(2,1)S(1)}, u32[]{:S(2)}, u32[]{:S(2)}) collective-permute-start(bf16[128,1024]{1,0:T(8,128)(2,1)S(1)} %shard_map.56), channel_id=1, source_target_pairs={{0,10},{1,11},{2,8},{3,9},{4,14},{5,15},{6,12},{7,13},{8,18},{9,19... | collective-permute-start | bytes 786440 | tf_op jit(solution)/shard_map/ppermute | solution.py:33
  74.0 21.1 %collective-permute-start.13 = (bf16[128,1024]{1,0:T(8,128)(2,1)S(1)}, bf16[128,1024]{1,0:T(8,128)(2,1)S(1)}, u32[]{:S(2)}, u32[]{:S(2)}) collective-permute-start(bf16[128,1024]{1,0:T(8,128)(2,1)S(1)} %collective-permute-done.9.refs_0_), channel_id=1, source_target_pairs={{0,16},{1,17},{2,18},{3,19},{4,20},{5,21},{6,22},{7,23},{8,24},{9,... | collective-permute-start | bytes 786440 | tf_op jit(solution)/shard_map/ppermute | solution.py:33
  76.7 18.4 %collective-permute-start.12 = (bf16[128,1024]{1,0:T(8,128)(2,1)S(1)}, bf16[128,1024]{1,0:T(8,128)(2,1)}, u32[]{:S(2)}, u32[]{:S(2)}) collective-permute-start(bf16[128,1024]{1,0:T(8,128)(2,1)S(1)} %collective-permute-done.9.refs_0_), channel_id=1, source_target_pairs={{0,24},{1,25},{2,26},{3,27},{4,28},{5,29},{6,30},{7,31},{8,0},{9,1... | collective-permute-start | bytes 786440 | tf_op jit(solution)/shard_map/ppermute | solution.py:33
  78.8 16.3 %collective-permute-start.11 = (bf16[128,1024]{1,0:T(8,128)(2,1)S(1)}, bf16[128,1024]{1,0:T(8,128)(2,1)}, u32[]{:S(2)}, u32[]{:S(2)}) collective-permute-start(bf16[128,1024]{1,0:T(8,128)(2,1)S(1)} %collective-permute-done.9.refs_0_), channel_id=1, source_target_pairs={{0,8},{1,9},{2,10},{3,11},{4,12},{5,13},{6,14},{7,15},{8,16},{9,17... | collective-permute-start | bytes 786440 | tf_op jit(solution)/shard_map/ppermute | solution.py:33
  96.2 38.7 %collective-permute-start.17 = (bf16[512,1024]{1,0:T(8,128)(2,1)S(1)}, bf16[512,1024]{1,0:T(8,128)(2,1)S(1)}, u32[]{:S(2)}, u32[]{:S(2)}) collective-permute-start(bf16[512,1024]{1,0:T(8,128)(2,1)S(1)} %pad_maximum_fusion.2), channel_id=1, source_target_pairs={{0,4},{4,0},{8,12},{12,8},{16,20},{20,16},{24,28},{28,24},{1,5},{5... | collective-permute-start | bytes 3145736 | tf_op jit(solution)/shard_map/ppermute | solution.py:24
  111.3 17.9 %collective-permute-start.15 = (bf16[128,1024]{1,0:T(8,128)(2,1)S(1)}, bf16[128,1024]{1,0:T(8,128)(2,1)S(1)}, u32[]{:S(2)}, u32[]{:S(2)}) collective-permute-start(bf16[128,1024]{1,0:T(8,128)(2,1)S(1)} %shard_map.60), channel_id=1, source_target_pairs={{0,2},{1,3},{2,0},{3,1},{4,6},{5,7},{6,4},{7,5},{8,10},{9,11},{10,... | collective-permute-start | bytes 786440 | tf_op jit(solution)/shard_map/ppermute | solution.py:24
  112.9 17.6 %collective-permute-start.20 = (bf16[80,1024]{1,0:T(8,128)(2,1)S(1)}, bf16[80,1024]{1,0:T(8,128)(2,1)S(1)}, u32[]{:S(2)}, u32[]{:S(2)}) collective-permute-start(bf16[80,1024]{1,0:T(8,128)(2,1)S(1)} %slice.25), channel_id=1, source_target_pairs={{0,18},{1,19},{2,16},{3,17},{4,22},{5,23},{6,20},{7,21},{8,26},{9,... | collective-permute-start | bytes 491528 | tf_op jit(solution)/shard_map/ppermute | solution.py:33
  115.5 15.1 %collective-permute-start.19 = (bf16[80,1024]{1,0:T(8,128)(2,1)S(1)}, bf16[80,1024]{1,0:T(8,128)(2,1)S(1)}, u32[]{:S(2)}, u32[]{:S(2)}) collective-permute-start(bf16[80,1024]{1,0:T(8,128)(2,1)S(1)} %slice.25), channel_id=1, source_target_pairs={{0,26},{1,27},{2,24},{3,25},{4,30},{5,31},{6,28},{7,29},{8,2},{9,3... | collective-permute-start | bytes 491528 | tf_op jit(solution)/shard_map/ppermute | solution.py:33
  117.8 12.8 %collective-permute-start.18 = (bf16[80,1024]{1,0:T(8,128)(2,1)S(1)}, bf16[80,1024]{1,0:T(8,128)(2,1)S(1)}, u32[]{:S(2)}, u32[]{:S(2)}) collective-permute-start(bf16[80,1024]{1,0:T(8,128)(2,1)S(1)} %slice.25), channel_id=1, source_target_pairs={{0,10},{1,11},{2,8},{3,9},{4,14},{5,15},{6,12},{7,13},{8,18},{9,19... | collective-permute-start | bytes 491528 | tf_op jit(solution)/shard_map/ppermute | solution.py:33
  129.1 5.8 %collective-permute-start.16 = (bf16[48,1024]{1,0:T(8,128)(2,1)S(1)}, bf16[48,1024]{1,0:T(8,128)(2,1)S(1)}, u32[]{:S(2)}, u32[]{:S(2)}) collective-permute-start(bf16[48,1024]{1,0:T(8,128)(2,1)S(1)} %slice.24), channel_id=1, source_target_pairs={{0,4},{4,0},{8,12},{12,8},{16,20},{20,16},{24,28},{28,24},{1,5},{5... | collective-permute-start | bytes 294920 | tf_op jit(solution)/shard_map/ppermute | solution.py:24
  135.0 18.8 %collective-permute-start.21 = (bf16[320,1024]{1,0:T(8,128)(2,1)S(1)}, bf16[320,1024]{1,0:T(8,128)(2,1)S(1)}, u32[]{:S(2)}, u32[]{:S(2)}) collective-permute-start(bf16[320,1024]{1,0:T(8,128)(2,1)S(1)} %pad_maximum_fusion.3), channel_id=1, source_target_pairs={{0,4},{4,0},{8,12},{12,8},{16,20},{20,16},{24,28},{28,24},{1,5},{5... | collective-permute-start | bytes 1966088 | tf_op jit(solution)/shard_map/ppermute | solution.py:24
  136.4 17.3 %collective-permute-start.24 = (bf16[96,1024]{1,0:T(8,128)(2,1)S(1)}, bf16[96,1024]{1,0:T(8,128)(2,1)S(1)}, u32[]{:S(2)}, u32[]{:S(2)}) collective-permute-start(bf16[96,1024]{1,0:T(8,128)(2,1)S(1)} %pad_maximum_fusion.4.refs_10_), channel_id=1, source_target_pairs={{0,16},{1,17},{2,18},{3,19},{4,20},{5,21},{6,22},{7,23},{8,24},{9,... | collective-permute-start | bytes 589832 | tf_op jit(solution)/shard_map/ppermute | solution.py:33
  136.5 17.3 %collective-permute-start.23 = (bf16[96,1024]{1,0:T(8,128)(2,1)S(1)}, bf16[96,1024]{1,0:T(8,128)(2,1)S(1)}, u32[]{:S(2)}, u32[]{:S(2)}) collective-permute-start(bf16[96,1024]{1,0:T(8,128)(2,1)S(1)} %pad_maximum_fusion.4.refs_10_), channel_id=1, source_target_pairs={{0,24},{1,25},{2,26},{3,27},{4,28},{5,29},{6,30},{7,31},{8,0},{9,1... | collective-permute-start | bytes 589832 | tf_op jit(solution)/shard_map/ppermute | solution.py:33
  140.1 13.6 %collective-permute-start.22 = (bf16[96,1024]{1,0:T(8,128)(2,1)S(1)}, bf16[96,1024]{1,0:T(8,128)(2,1)S(1)}, u32[]{:S(2)}, u32[]{:S(2)}) collective-permute-start(bf16[96,1024]{1,0:T(8,128)(2,1)S(1)} %pad_maximum_fusion.4.refs_10_), channel_id=1, source_target_pairs={{0,8},{1,9},{2,10},{3,11},{4,12},{5,13},{6,14},{7,15},{8,16},{9,17... | collective-permute-start | bytes 589832 | tf_op jit(solution)/shard_map/ppermute | solution.py:33
  (18 other events, 251.1 us)
